TPU v7x, 128 devices: a whole 4x4x4 slice. The times are simulated.
128 devices in a mesh: dom: 32 (over z, y, core), sub: 4 (over x).
Axes of the slice: x: 4, y: 4, z: 4, core: 2. Of those that a mesh axis runs over, the one named last changes fastest.
Arguments:
- displacement: float32 [3, 512, 289], P(None, ('dom', 'sub')), may hold values from -6 to 6
- macro_modulus: float32 [8, 131072], P(None, ('dom', 'sub')), may hold values from 0.5 to 4
- damaged_count: int32 [128], P(('dom', 'sub')), may hold values from 1 to 64, 4096 in all
- damaged_points: int32 [128, 64], P(('dom', 'sub')), may hold values from 0 to 8191, as said below
- damage: bfloat16 [8192, 4096], P(('dom', 'sub')), may hold values from 0 to 0.59765625
- voxel_modulus: bfloat16 [8192, 4096], P(('dom', 'sub')), may hold values from 0.5 to 4
Outputs:
- nodal_force: float32 [3, 512, 289], P(None, ('dom', 'sub'))
- new_damage: bfloat16 [8192, 4096], P(('dom', 'sub'))
Inputs may be any that keep to these rules, and one draw needn't show every extreme that they name: `damaged_count`: the counts of all partitions sum to 4096, and the largest is 64. `damaged_points`: each row names 64 different points of its partition; the first damaged_count of them are the damaged ones; partition 0 lists point 0 and point 8 * 4 * 16^2 - 1.
All inputs are finite; a program needn't handle non-finite values. No bound on the sum of `damaged_count` on one device may be relied on, other than what follows from the above.
Results may differ from a plain program's by a relative error of at most 0.0055.
Values may be sent and summed in bfloat16 or wider, within the bound.
No kernel may reach another device: no remote copies, remote signals or barrier semaphores. Data moves between devices by JAX's collectives and lax.ppermute only.
A program may use at most 64 MiB of HBM per device.

v0:
```python
import math

import jax
import jax.numpy as jnp
import ml_dtypes
import numpy as np
from jax import lax
from jax.experimental import pallas as pl
from jax.experimental.pallas import tpu as pltpu
from jax.sharding import PartitionSpec as P

CELL = 16
EXY = 16
VOX = 4096
SLOTS = 64
GROUP = 16
LAYERS = 4
NODES = 289
WIDE = 384
ROW = EXY + 1

lam_hat = 0.2 / 0.72
mu_hat = 1.0 / 2.4
ref_modulus = 2.0
kappa_sq = 4.0
voigt_pairs = ((0, 0), (1, 1), (2, 2), (1, 2), (0, 2), (0, 1))
odd_in_x = (False, False, False, False, True, True)
table_scale = 1.132805
entry_pairs = [(k, m) for k in range(6) for m in range(k, 6)]
f32 = jnp.float32
bf16 = jnp.bfloat16
shifts = (0, 1, ROW, ROW + 1)


def shape_table():
    gauss_coord = 1.0 / math.sqrt(3.0)
    gradients = np.zeros((8, 8, 3), np.float32)
    for corner in range(8):
        signs = [2 * (corner >> d & 1) - 1 for d in range(3)]
        for gauss_no in range(8):
            coords = [(2 * (gauss_no >> d & 1) - 1) * gauss_coord for d in range(3)]
            factor = [(1.0 + signs[d] * coords[d]) / 2.0 for d in range(3)]
            for direction in range(3):
                value = float(signs[direction])
                for other in range(3):
                    if other != direction:
                        value = value * factor[other]
                gradients[corner, gauss_no, direction] = value
    return gradients


def macro_tables():
    gradients = shape_table().astype(np.float64)
    strain = np.zeros((LAYERS, 6, 8, 3, 4, 8))
    force = np.zeros((3, 4, 8, LAYERS, 6, 8))
    for layer in range(LAYERS):
        for corner in range(8):
            node_layer = layer + (corner >> 2)
            row = 4 if node_layer == 0 else node_layer - 1
            shift = corner & 3
            for k, (a, b) in enumerate(voigt_pairs):
                strain[layer, k, :, a, shift, row] += 0.5 * gradients[corner, :, b]
                strain[layer, k, :, b, shift, row] += 0.5 * gradients[corner, :, a]
                force[a, shift, row, layer, k, :] += 0.125 * gradients[corner, :, b]
                if a != b:
                    force[b, shift, row, layer, k, :] += 0.125 * gradients[corner, :, a]
    return (
        strain.reshape(LAYERS * 48, 96).astype(np.float32),
        force.reshape(96, LAYERS * 48).astype(np.float32),
    )


def spread_table():
    table = np.zeros((EXY * EXY, WIDE), np.float32)
    for y in range(EXY):
        for x in range(EXY):
            table[y * EXY + x, y * ROW + x] = 1.0
    return table


def green_matrix(n):
    n = np.asarray(n, np.float64)
    m = n @ n
    out = np.zeros((6, 6))
    if m == 0:
        return out
    lam_ref, mu_ref = ref_modulus * lam_hat, ref_modulus * mu_hat
    coupling = (lam_ref + mu_ref) / (mu_ref * (lam_ref + 2.0 * mu_ref))
    for col, (a, b) in enumerate(voigt_pairs):
        t = np.zeros((3, 3))
        t[a, b] = t[b, a] = 1.0
        u = t @ n
        amp = u / (mu_ref * m) - coupling * (n @ u) * n / m**2
        for k, (c, d) in enumerate(voigt_pairs):
            out[k, col] = 0.5 * (n[c] * amp[d] + n[d] * amp[c])
    return out


def lane_modes():
    modes = []
    for kz in range(1, 8):
        for ky in range(16):
            modes += [(ky, kz, 0), (ky, kz, 1)]
    for kz in (0, 8):
        for ky in range(1, 8):
            modes += [(ky, kz, 0), (ky, kz, 1)]
        modes += [(0, kz, 2), (8, kz, 2)]
    return modes


def spectral_tables():
    side = np.arange(16)
    modes = lane_modes()
    y, z = side.repeat(16), np.tile(side, 16)
    first = np.zeros((256, 256))
    second = np.zeros((256, 256))
    weight = np.zeros(256)
    for lane, (ky, kz, kind) in enumerate(modes):
        phase = 2 * np.pi * ((y * ky + z * kz) % 16) / 16
        first[:, lane] = np.sin(phase) if kind == 1 else np.cos(phase)
        second[:, lane] = (-np.sin(phase), np.cos(phase), np.cos(phase))[kind]
        weight[lane] = 1.0 if kind == 2 else 2.0
    rows = np.zeros((16, 16))
    row_weight = np.full(16, 2.0)
    row_weight[[0, 8]] = 1.0
    for row in range(16):
        k = row if row < 9 else row - 8
        phase = 2 * np.pi * (side * k % 16) / 16
        rows[row] = np.cos(phase) if row < 9 else np.sin(phase)

    def rounded(table):
        table = np.where(np.abs(table) < 1e-9, 0.0, table)
        return (table * table_scale).astype(ml_dtypes.bfloat16)

    eye = np.eye(GROUP)
    forward_x = rounded(np.kron(rows, eye))
    inverse_x = rounded(np.kron((rows * row_weight[:, None]).T, eye))
    signed = np.where(side < 8, side, side - 16)

    def green_at(kx, ky, kz):
        own = green_matrix((signed[kx], signed[ky], kz))
        if kz in (0, 8):
            own = (own + green_matrix((signed[-kx % 16], signed[-ky % 16], kz))) / 2
        return own

    green = np.zeros((9, len(entry_pairs), 256))
    double = np.array([1, 1, 1, 2, 2, 2])
    for kx in range(9):
        for lane, (ky, kz, kind) in enumerate(modes):
            matrix = green_at(kx, ky, kz) / double[None, :]
            green[kx, :, lane] = [matrix[pair] for pair in entry_pairs]
    green /= table_scale**4 * VOX
    return (
        forward_x,
        inverse_x,
        rounded(first),
        rounded(second),
        rounded((first * weight).T),
        rounded((second * weight).T),
        green.astype(np.float32),
    )


def dot(a, b, dims=((1,), (0,)), precision=None):
    return lax.dot_general(a, b, (dims, ((), ())), precision=precision, preferred_element_type=f32)


def split(value, parts):
    out = []
    for _ in range(parts):
        out.append(value.astype(bf16))
        value = value - out[-1].astype(f32)
    return out


def table_split(table, order):
    parts, rest = [], table.astype(np.float64)
    for _ in range(3):
        parts.append(rest.astype(ml_dtypes.bfloat16))
        rest = rest - parts[-1].astype(np.float64)
    return np.concatenate([parts[i] for i in order], axis=1)


def split_dot(table, value, order):
    parts = split(value, max(order) + 1)
    return dot(table, jnp.concatenate([parts[i] for i in order], axis=0))


fine_table, fine_value = (0, 0, 1, 0, 1, 2), (0, 1, 0, 2, 1, 0)
half_table, half_value = (0, 1, 0), (0, 0, 1)


def strain_law(s):
    trace = lam_hat * (s[0] + s[1] + s[2])
    return [2.0 * mu_hat * s[k] + trace if k < 3 else 2.0 * mu_hat * s[k] for k in range(6)]


def strain_energy(s):
    return s[0] * s[0] + s[1] * s[1] + s[2] * s[2] + 2.0 * (s[3] * s[3] + s[4] * s[4] + s[5] * s[5])


def cell_kernel(
    count_ref,
    disp_hbm,
    below_hbm,
    modulus_hbm,
    points_hbm,
    damage_hbm,
    voxel_hbm,
    matrix_hbm,
    green_hbm,
    strain_hbm,
    force_hbm,
    spread_hbm,
    own_ref,
    low_ref,
    new_hbm,
    disp_ref,
    below_ref,
    modulus_ref,
    points_ref,
    damage_ref,
    voxel_ref,
    matrix_ref,
    green_ref,
    strain_ref,
    force_ref,
    spread_ref,
    in_sems,
    out_sems,
    new_ref,
    nodes_ref,
    macro_ref,
    total_ref,
    polar_ref,
    cos_ref,
    sin_ref,
    spec_cos_ref,
    spec_sin_ref,
    green_cos_ref,
    green_sin_ref,
    plane_ref,
    field_ref,
):
    count = count_ref[0]
    pairs = [
        (disp_hbm, disp_ref),
        (below_hbm, below_ref),
        (strain_hbm, strain_ref),
        (points_hbm, points_ref),
        (damage_hbm, damage_ref),
        (voxel_hbm, voxel_ref),
        (matrix_hbm, matrix_ref),
        (green_hbm, green_ref),
        (modulus_hbm, modulus_ref),
        (spread_hbm, spread_ref),
        (force_hbm, force_ref),
    ]
    copies = [
        pltpu.make_async_copy(source, target, in_sems.at[i])
        for i, (source, target) in enumerate(pairs)
    ]
    for copy in copies:
        copy.start()
    forward_x_ref, inverse_x_ref, first_ref, second_ref, first_back_ref, second_back_ref = [
        matrix_ref.at[i] for i in range(6)
    ]
    nodes_ref[...] = jnp.zeros(nodes_ref.shape, f32)
    for copy in copies[:4]:
        copy.wait()
    for i in range(3):
        nodes_ref[i, 0:LAYERS, 0:NODES] = disp_ref[i]
        nodes_ref[i, LAYERS : LAYERS + 1, 0:NODES] = below_ref[i, LAYERS - 1 : LAYERS]
    rolled = []
    for i in range(3):
        rows = nodes_ref[i]
        for shift in shifts:
            rolled.append(rows if shift == 0 else pltpu.roll(rows, WIDE - shift, 1))
    strain = split_dot(strain_ref[...], jnp.concatenate(rolled, axis=0), fine_value)
    points = points_ref[...]
    gauss = points // (LAYERS * EXY * EXY)
    layer = points // (EXY * EXY) % LAYERS
    lane = points % (EXY * EXY) // EXY * ROW + points % EXY
    lane_no = lax.broadcasted_iota(jnp.int32, (WIDE, SLOTS), 0)
    where_at = [
        ((lane_no == lane) & (layer == z)).astype(f32).astype(bf16) for z in range(LAYERS)
    ]
    gauss_no = lax.broadcasted_iota(jnp.int32, (8, SLOTS), 0)
    is_gauss = gauss_no == gauss
    picked = sum(dot(strain[z * 48 : z * 48 + 48].astype(bf16), where_at[z]) for z in range(LAYERS))
    for k in range(6):
        mine = jnp.where(is_gauss, picked[k * 8 : k * 8 + 8], 0.0).astype(bf16)
        macro_ref[k] = dot(mine, jnp.ones((8, 128), bf16), ((0,), (0,)))

    for copy in copies[4:8]:
        copy.wait()

    def store(block, source):
        cells = pl.ds(pl.multiple_of(block * GROUP, GROUP), GROUP)
        return pltpu.make_async_copy(source.at[cells], new_hbm.at[cells], out_sems.at[block])

    def solve(block):
        base = pl.multiple_of(block * GROUP, GROUP)
        cells = pl.ds(base, GROUP)

        def tiles():
            for x in range(CELL):
                for half in range(2):
                    at = pl.ds(x * 256 + half * 128, 128)
                    rows = pl.ds(x * GROUP, GROUP)
                    lanes = pl.ds(half * 128, 128)
                    yield at, rows, lanes

        def forward(parts):
            for k in range(parts):
                both = dot(forward_x_ref[...], polar_ref[k]).astype(bf16)
                cos_ref[k] = both[: 9 * GROUP]
                sin_ref[k] = both[9 * GROUP :]
            shape_cos, shape_sin = (parts * 9 * GROUP, 256), (parts * 7 * GROUP, 256)
            spec_cos_ref[0:parts] = dot(
                cos_ref[0:parts].reshape(shape_cos), first_ref[...]
            ).reshape(parts, 9 * GROUP, 256)
            spec_sin_ref[0:parts] = dot(
                sin_ref[0:parts].reshape(shape_sin), second_ref[...]
            ).reshape(parts, 7 * GROUP, 256)

        def green_rows(load_cos, load_sin):
            for half in range(2):
                lanes = pl.ds(half * 128, 128)
                for kx in range(9):
                    table = {}
                    for entry, (k, m) in enumerate(entry_pairs):
                        if kx == 0 and odd_in_x[k] != odd_in_x[m]:
                            continue
                        table[k, m] = table[m, k] = green_ref[kx, entry : entry + 1, lanes]

                    def apply(v):
                        return [
                            sum(table[k, m] * v[m] for m in range(6) if (k, m) in table)
                            for k in range(6)
                        ]

                    rows = pl.ds(kx * GROUP, GROUP)
                    a = load_cos(rows, lanes)
                    if kx in (0, 8):
                        a = apply(a)
                        for k in range(6):
                            green_cos_ref[k, rows, lanes] = a[k].astype(bf16)
                        continue
                    rows_sin = pl.ds((kx - 1) * GROUP, GROUP)
                    c = load_sin(rows_sin, lanes)
                    one = apply([c[k] if odd_in_x[k] else a[k] for k in range(6)])
                    two = apply([a[k] if odd_in_x[k] else c[k] for k in range(6)])
                    for k in range(6):
                        cos_part, sin_part = (two, one) if odd_in_x[k] else (one, two)
                        green_cos_ref[k, rows, lanes] = cos_part[k].astype(bf16)
                        green_sin_ref[k, rows_sin, lanes] = sin_part[k].astype(bf16)

        def backward():
            plane_ref[:, 0 : 9 * GROUP] = (
                dot(green_cos_ref[...].reshape(54 * GROUP, 256), first_back_ref[...])
                .astype(bf16)
                .reshape(6, 9 * GROUP, 256)
            )
            plane_ref[:, 9 * GROUP :] = (
                dot(green_sin_ref[...].reshape(42 * GROUP, 256), second_back_ref[...])
                .astype(bf16)
                .reshape(6, 7 * GROUP, 256)
            )
            for k in range(6):
                field_ref[k] = dot(inverse_x_ref[...], plane_ref[k])

        macro = [macro_ref[k, cells, :] for k in range(6)]
        energy = strain_energy(macro)
        uniform = energy / (energy + kappa_sq)
        for at, rows, lanes in tiles():
            old = damage_ref[cells, at].astype(f32)
            young = voxel_ref[cells, at].astype(f32)
            excess = (1.0 - jnp.maximum(old, uniform)) * young - ref_modulus
            polar_ref[0, rows, lanes] = excess.astype(bf16)
        forward(1)
        inner = strain_law(macro)
        inner = [inner[k] if k < 3 else 2.0 * inner[k] for k in range(6)]

        def scaled(ref):
            def load(rows, lanes):
                value = ref[0, rows, lanes]
                return [value * inner[k] for k in range(6)]

            return load

        green_rows(scaled(spec_cos_ref), scaled(spec_sin_ref))
        backward()
        for at, rows, lanes in tiles():
            s = [macro[k] - field_ref[k, rows, lanes] for k in range(6)]
            old = damage_ref[cells, at].astype(f32)
            young = voxel_ref[cells, at].astype(f32)
            energy = strain_energy(s)
            now = jnp.maximum(old, energy / (energy + kappa_sq))
            excess = (1.0 - now) * young - ref_modulus
            polar = strain_law(s)
            for k in range(6):
                value = polar[k] * excess
                polar_ref[k, rows, lanes] = (value if k < 3 else 2.0 * value).astype(bf16)
        forward(6)

        def plain(ref):
            return lambda rows, lanes: [ref[k, rows, lanes] for k in range(6)]

        green_rows(plain(spec_cos_ref), plain(spec_sin_ref))
        backward()
        slot_no = lax.broadcasted_iota(jnp.int32, (GROUP, 128), 0) + base
        live = slot_no < count
        sums = [jnp.zeros((GROUP, 128), f32) for k in range(6)]
        for at, rows, lanes in tiles():
            s = [macro[k] - field_ref[k, rows, lanes] for k in range(6)]
            old = damage_ref[cells, at].astype(f32)
            young = voxel_ref[cells, at].astype(f32)
            energy = strain_energy(s)
            now = jnp.maximum(old, energy / (energy + kappa_sq))
            kept = (1.0 - now) * young
            sums = [sums[k] + kept * s[k] for k in range(6)]
            new_ref[cells, at] = jnp.where(live, now, old).astype(bf16)
        for k in range(6):
            total_ref[k, cells, :] = sums[k]

    busy = (count + GROUP - 1) // GROUP

    @pl.loop(busy, SLOTS // GROUP)
    def _(block):
        store(block, damage_ref).start()

    @pl.loop(0, busy)
    def _(block):
        solve(block)
        store(block, new_ref).start()

    for copy in copies[8:]:
        copy.wait()

    slot_live = lax.broadcasted_iota(jnp.int32, (8, SLOTS), 1) < count
    at_point = is_gauss & slot_live
    ones = jnp.ones((8, 384), bf16)
    mean = [
        dot(ones, jnp.concatenate(split(total_ref[k], 3), axis=1), ((1,), (1,))) * (1.0 / VOX)
        for k in range(6)
    ]
    cell_stress = [
        jnp.where(at_point, value, 0.0).astype(bf16).astype(f32) for value in strain_law(mean)
    ]
    cell_stress.append(at_point.astype(f32))
    cell_stress = jnp.concatenate(cell_stress, axis=0).astype(bf16)
    compact = [modulus_ref[:, z * 256 : z * 256 + 256] for z in range(LAYERS)]
    young_parts = dot(jnp.concatenate(split(jnp.concatenate(compact, axis=0), 3), axis=0), spread_ref[...])
    young_all = young_parts[0:32] + young_parts[32:64] + young_parts[64:96]
    stress = []
    for z in range(LAYERS):
        young = young_all[z * 8 : z * 8 + 8]
        from_cells = dot(cell_stress, where_at[z], ((1,), (1,)))
        from_cell = from_cells[48:56] > 0.5
        elastic = strain_law([strain[z * 48 + k * 8 : z * 48 + k * 8 + 8] for k in range(6)])
        for k in range(6):
            stress.append(jnp.where(from_cell, from_cells[k * 8 : k * 8 + 8], young * elastic[k]))
    forces = split_dot(force_ref[...], jnp.concatenate(stress, axis=0), half_value)
    for i in range(3):
        total = 0.0
        for corner, shift in enumerate(shifts):
            part = forces[(i * 4 + corner) * 8 : (i * 4 + corner) * 8 + 8]
            total = total + (part if shift == 0 else pltpu.roll(part, shift, 1))
        own_ref[i] = total[0:LAYERS, 0:NODES]
        low_ref[i, 0 : LAYERS - 1] = jnp.zeros((LAYERS - 1, NODES), f32)
        low_ref[i, LAYERS - 1 : LAYERS] = total[LAYERS : LAYERS + 1, 0:NODES]

    @pl.loop(0, SLOTS // GROUP)
    def _(block):
        store(block, new_ref).wait()


def partition_step(displacement, below, modulus, count, points, damage, voxel):
    *matrices, green = spectral_tables()
    strain, force = macro_tables()
    operands = [
        displacement,
        below,
        modulus,
        points,
        damage,
        voxel,
        jnp.asarray(np.stack(matrices)),
        jnp.asarray(green),
        jnp.asarray(table_split(strain, fine_table)),
        jnp.asarray(table_split(force, half_table)),
        jnp.asarray(spread_table().astype(ml_dtypes.bfloat16)),
    ]
    anywhere = pl.BlockSpec(memory_space=pl.ANY)
    shape = (3, LAYERS, NODES)
    return pl.pallas_call(
        cell_kernel,
        in_specs=[pl.BlockSpec(memory_space=pltpu.SMEM)] + [anywhere] * len(operands),
        out_specs=[pl.BlockSpec(shape), pl.BlockSpec(shape), anywhere],
        out_shape=[
            jax.ShapeDtypeStruct(shape, f32),
            jax.ShapeDtypeStruct(shape, f32),
            jax.ShapeDtypeStruct((SLOTS, VOX), bf16),
        ],
        scratch_shapes=[pltpu.VMEM(x.shape, x.dtype) for x in operands]
        + [
            pltpu.SemaphoreType.DMA((len(operands),)),
            pltpu.SemaphoreType.DMA((SLOTS // GROUP,)),
            pltpu.VMEM((SLOTS, VOX), bf16),
            pltpu.VMEM((3, 8, WIDE), f32),
            pltpu.VMEM((6, SLOTS, 128), f32),
            pltpu.VMEM((6, SLOTS, 128), f32),
            pltpu.VMEM((6, 256, 256), bf16),
            pltpu.VMEM((6, 9 * GROUP, 256), bf16),
            pltpu.VMEM((6, 7 * GROUP, 256), bf16),
            pltpu.VMEM((6, 9 * GROUP, 256), f32),
            pltpu.VMEM((6, 7 * GROUP, 256), f32),
            pltpu.VMEM((6, 9 * GROUP, 256), bf16),
            pltpu.VMEM((6, 7 * GROUP, 256), bf16),
            pltpu.VMEM((6, 256, 256), bf16),
            pltpu.VMEM((6, 256, 256), f32),
        ],
        compiler_params=pltpu.CompilerParams(vmem_limit_bytes=48 * 1024 * 1024),
        name="pier_step",
    )(count, *operands)


def shifted(value, steps):
    axes = ("dom", "sub")
    total = lax.axis_size(axes)
    pairs = [(i, i + steps) for i in range(total) if 0 <= i + steps < total]
    return lax.ppermute(value, axes, pairs)


def body(displacement, modulus, count, points, damage, voxel):
    below = shifted(displacement, 1)
    own, low, new_damage = partition_step(
        displacement, below, modulus, count, points, damage, voxel
    )
    return own + shifted(low, -1), new_damage


def solution(mesh):
    return jax.shard_map(
        body,
        mesh=mesh,
        in_specs=(
            P(None, ("dom", "sub"), None),
            P(None, ("dom", "sub")),
            P(("dom", "sub")),
            P(("dom", "sub"), None),
            P(("dom", "sub"), None),
            P(("dom", "sub"), None),
        ),
        out_specs=(P(None, ("dom", "sub"), None), P(("dom", "sub"), None)),
        check_vma=False,
    )
```

profile of v0, /device:TPU:32, one launch (start us, length us, event | category | flops | bytes accessed | tf_op | source)
XLA Modules:
  0.0 43.5 jit_solution(18291498621526594137)
XLA Ops:
  0.6 0.0 copy-start.9
  0.6 3.4 %collective-permute-start = (f32[3,4,289]{2,1,0:T(4,128)}, f32[3,4,289]{2,1,0:T(4,128)S(1)}, u32[]{:S(2)}, u32[]{:S(2)}) collective-permute-start(f32[3,4,289]{2,1,0:T(4,128)} %disp_hbm.1), channel_id=1, source_target_pairs={{0,1},{1,2},{2,3},{3,4},{4,5},{5,6},{6,7},{7,8},{8,9},{9,10},{10,1... | collective-permute-start | bytes 41624 | tf_op jit(solution)/shard_map/ppermute | solution.py:533
  4.7 5.5 %collective-permute-done.below_hbm = f32[3,4,289]{2,1,0:T(4,128)S(1)} collective-permute-done((f32[3,4,289]{2,1,0:T(4,128)}, f32[3,4,289]{2,1,0:T(4,128)S(1)}, u32[]{:S(2)}, u32[]{:S(2)}) %collective-permute-start) | collective-permute-done | bytes 13904 | tf_op jit(solution)/shard_map/ppermute | solution.py:533
  10.2 0.0 copy-done.9
  10.2 0.0 copy-start
  10.2 1.1 %copy-done = bf16[6,256,256]{2,1,0:T(8,128)(2,1)S(1)} copy-done((bf16[6,256,256]{2,1,0:T(8,128)(2,1)S(1)}, bf16[6,256,256]{2,1,0:T(8,128)(2,1)}, u32[]{:S(2)}) %copy-start) | copy-done | bytes 786456
  11.3 0.0 copy-start.1
  11.3 1.0 %copy-done.1 = bf16[64,4096]{1,0:T(8,128)(2,1)S(1)} copy-done((bf16[64,4096]{1,0:T(8,128)(2,1)S(1)}, bf16[64,4096]{1,0:T(8,128)(2,1)}, u32[]{:S(2)}) %copy-start.1) | copy-done | bytes 524312
  12.3 0.0 copy-start.2
  12.3 1.0 %copy-done.2 = bf16[64,4096]{1,0:T(8,128)(2,1)S(1)} copy-done((bf16[64,4096]{1,0:T(8,128)(2,1)S(1)}, bf16[64,4096]{1,0:T(8,128)(2,1)}, u32[]{:S(2)}) %copy-start.2) | copy-done | bytes 524312
  13.4 0.0 copy-start.3
  13.4 0.9 %copy-done.3 = bf16[192,576]{1,0:T(8,128)(2,1)S(1)} copy-done((bf16[192,576]{1,0:T(8,128)(2,1)S(1)}, bf16[192,576]{1,0:T(8,128)(2,1)}, u32[]{:S(2)}) %copy-start.3) | copy-done | bytes 221208
  14.3 0.0 copy-start.4
  14.3 0.9 %copy-done.4 = f32[9,21,256]{2,1,0:T(8,128)S(1)} copy-done((f32[9,21,256]{2,1,0:T(8,128)S(1)}, f32[9,21,256]{2,1,0:T(8,128)}, u32[]{:S(2)}) %copy-start.4) | copy-done | bytes 193560
  15.3 0.0 copy-start.5
  15.3 0.9 %copy-done.5 = bf16[256,384]{1,0:T(8,128)(2,1)S(1)} copy-done((bf16[256,384]{1,0:T(8,128)(2,1)S(1)}, bf16[256,384]{1,0:T(8,128)(2,1)}, u32[]{:S(2)}) %copy-start.5) | copy-done | bytes 196632
  16.2 0.0 copy-start.6
  16.2 0.9 %copy-done.6 = bf16[96,576]{1,0:T(8,128)(2,1)S(1)} copy-done((bf16[96,576]{1,0:T(8,128)(2,1)S(1)}, bf16[96,576]{1,0:T(8,128)(2,1)}, u32[]{:S(2)}) %copy-start.6) | copy-done | bytes 110616
  17.1 0.0 copy-start.7
  17.1 0.8 %copy-done.7 = f32[8,1024]{1,0:T(8,128)S(1)} copy-done((f32[8,1024]{1,0:T(8,128)S(1)}, f32[8,1024]{1,0:T(8,128)}, u32[]{:S(2)}) %copy-start.7) | copy-done | bytes 32792
  17.8 0.0 copy-start.8
  17.8 0.7 %copy-done.8 = f32[3,4,289]{2,1,0:T(4,128)S(1)} copy-done((f32[3,4,289]{2,1,0:T(4,128)S(1)}, f32[3,4,289]{2,1,0:T(4,128)}, u32[]{:S(2)}) %copy-start.8) | copy-done | bytes 13896
  18.6 18.6 %pier_step.1 = (f32[3,4,289]{2,1,0:T(4,128)S(1)}, f32[3,4,289]{2,1,0:T(4,128)S(1)}, bf16[64,4096]{1,0:T(8,128)(2,1)}) custom-call(s32[1]{0:T(128)S(6)} %copy.13.count_ref, f32[3,4,289]{2,1,0:T(4,128)S(1)} %copy-done.8, f32[3,4,289]{2,1,0:T(4,128)S(1)} %collective-permute-done.below_hbm, f32[8,1024]{1,0:T(8,128)S(1)} %copy-done.7, s32[1,64]{1,0:T(1,128)S(1)} %copy-done.9, ...), custom_call_target="tpu_custom_call" | custom-call | tf_op jit(solution)/shard_map/pier_step/pallas_call | solution.py:497
  37.2 1.9 %collective-permute-start.1 = (f32[3,4,289]{2,1,0:T(4,128)S(1)}, f32[3,4,289]{2,1,0:T(4,128)S(1)}, u32[]{:S(2)}, u32[]{:S(2)}) collective-permute-start(f32[3,4,289]{2,1,0:T(4,128)S(1)} %get-tuple-element.6), channel_id=1, source_target_pairs={{1,0},{2,1},{3,2},{4,3},{5,4},{6,5},{7,6},{8,7},{9,8},{10,9},{11,1... | collective-permute-start | bytes 41624 | tf_op jit(solution)/shard_map/ppermute | solution.py:533
  39.1 3.7 %collective-permute-done.1 = f32[3,4,289]{2,1,0:T(4,128)S(1)} collective-permute-done((f32[3,4,289]{2,1,0:T(4,128)S(1)}, f32[3,4,289]{2,1,0:T(4,128)S(1)}, u32[]{:S(2)}, u32[]{:S(2)}) %collective-permute-start.1) | collective-permute-done | bytes 13904 | tf_op jit(solution)/shard_map/ppermute | solution.py:533
  42.9 0.6 %add.3 = f32[3,4,289]{2,1,0:T(4,128)} add(f32[3,4,289]{2,1,0:T(4,128)S(1)} %get-tuple-element.5, f32[3,4,289]{2,1,0:T(4,128)S(1)} %collective-permute-done.1) | non-fusion elementwise | flops 3468 | bytes 41616 | tf_op jit(solution)/shard_map/add | solution.py:541
Async XLA Ops:
  0.6 9.5 %copy-start.9 = (s32[1,64]{1,0:T(1,128)S(1)}, s32[1,64]{1,0:T(1,128)}, u32[]{:S(2)}) copy-start(s32[1,64]{1,0:T(1,128)} %points_hbm.1) | copy-start | bytes 772
  0.6 9.5 %collective-permute-start = (f32[3,4,289]{2,1,0:T(4,128)}, f32[3,4,289]{2,1,0:T(4,128)S(1)}, u32[]{:S(2)}, u32[]{:S(2)}) collective-permute-start(f32[3,4,289]{2,1,0:T(4,128)} %disp_hbm.1), channel_id=1, source_target_pairs={{0,1},{1,2},{2,3},{3,4},{4,5},{5,6},{6,7},{7,8},{8,9},{9,10},{10,1... | collective-permute-start | bytes 41624 | tf_op jit(solution)/shard_map/ppermute | solution.py:533
  10.2 1.1 %copy-start = (bf16[6,256,256]{2,1,0:T(8,128)(2,1)S(1)}, bf16[6,256,256]{2,1,0:T(8,128)(2,1)}, u32[]{:S(2)}) copy-start(bf16[6,256,256]{2,1,0:T(8,128)(2,1)} %constant.10.clone.matrix_hbm) | copy-start | bytes 2359300
  11.3 1.0 %copy-start.1 = (bf16[64,4096]{1,0:T(8,128)(2,1)S(1)}, bf16[64,4096]{1,0:T(8,128)(2,1)}, u32[]{:S(2)}) copy-start(bf16[64,4096]{1,0:T(8,128)(2,1)} %damage_hbm.1) | copy-start | bytes 1572868
  12.3 1.0 %copy-start.2 = (bf16[64,4096]{1,0:T(8,128)(2,1)S(1)}, bf16[64,4096]{1,0:T(8,128)(2,1)}, u32[]{:S(2)}) copy-start(bf16[64,4096]{1,0:T(8,128)(2,1)} %voxel_hbm.1) | copy-start | bytes 1572868
  13.4 0.9 %copy-start.3 = (bf16[192,576]{1,0:T(8,128)(2,1)S(1)}, bf16[192,576]{1,0:T(8,128)(2,1)}, u32[]{:S(2)}) copy-start(bf16[192,576]{1,0:T(8,128)(2,1)} %constant.12.clone.strain_hbm) | copy-start | bytes 663556
  14.3 0.9 %copy-start.4 = (f32[9,21,256]{2,1,0:T(8,128)S(1)}, f32[9,21,256]{2,1,0:T(8,128)}, u32[]{:S(2)}) copy-start(f32[9,21,256]{2,1,0:T(8,128)} %constant.11.clone.green_hbm) | copy-start | bytes 580612
  15.3 0.9 %copy-start.5 = (bf16[256,384]{1,0:T(8,128)(2,1)S(1)}, bf16[256,384]{1,0:T(8,128)(2,1)}, u32[]{:S(2)}) copy-start(bf16[256,384]{1,0:T(8,128)(2,1)} %constant.14.clone.spread_hbm) | copy-start | bytes 589828
  16.2 0.9 %copy-start.6 = (bf16[96,576]{1,0:T(8,128)(2,1)S(1)}, bf16[96,576]{1,0:T(8,128)(2,1)}, u32[]{:S(2)}) copy-start(bf16[96,576]{1,0:T(8,128)(2,1)} %constant.13.clone.force_hbm) | copy-start | bytes 331780
  17.1 0.8 %copy-start.7 = (f32[8,1024]{1,0:T(8,128)S(1)}, f32[8,1024]{1,0:T(8,128)}, u32[]{:S(2)}) copy-start(f32[8,1024]{1,0:T(8,128)} %modulus_hbm.1) | copy-start | bytes 98308
  17.8 0.7 %copy-start.8 = (f32[3,4,289]{2,1,0:T(4,128)S(1)}, f32[3,4,289]{2,1,0:T(4,128)}, u32[]{:S(2)}) copy-start(f32[3,4,289]{2,1,0:T(4,128)} %disp_hbm.1) | copy-start | bytes 41620
  37.2 5.7 %collective-permute-start.1 = (f32[3,4,289]{2,1,0:T(4,128)S(1)}, f32[3,4,289]{2,1,0:T(4,128)S(1)}, u32[]{:S(2)}, u32[]{:S(2)}) collective-permute-start(f32[3,4,289]{2,1,0:T(4,128)S(1)} %get-tuple-element.6), channel_id=1, source_target_pairs={{1,0},{2,1},{3,2},{4,3},{5,4},{6,5},{7,6},{8,7},{9,8},{10,9},{11,1... | collective-permute-start | bytes 41624 | tf_op jit(solution)/shard_map/ppermute | solution.py:533
where the time goes:
time: 44 us; the launch traced here: 43.5 us
  Pallas kernels  18.6 us (42%)
  waiting for transfers between devices  9.18 us (21%)
  local copies, waits for them, and re-layouts  8.41 us (19%)
  starting transfers between devices  5.32 us (12%)
  between operations  1.32 us (3%)
  other arithmetic  0.61 us (1%)
    pallas_call x1, Pallas kernels, partition_step(): pl.pallas_call(cell_kernel, in_specs=[pl.BlockSpec(memory_space=pltpu.SME...  18.6 us
    ppermute x2, waiting for transfers between devices, shifted(): return lax.ppermute(value, axes, pairs)  9.18 us
    unnamed x20, local copies, waits for them, and re-layouts  8.41 us
    ppermute x2, starting transfers between devices, shifted(): return lax.ppermute(value, axes, pairs)  5.32 us
  transfers between devices with their start and end apart: 2, of which 2 were waited for; matrix products, arithmetic and copies ran while one was open for 0% of the time, Pallas kernels for 0%

commit v1 on v0

--- a/solution.py
+++ b/solution.py
@@ -492,12 +492,12 @@
         jnp.asarray(table_split(force, half_table)),
         jnp.asarray(spread_table().astype(ml_dtypes.bfloat16)),
     ]
-    anywhere = pl.BlockSpec(memory_space=pl.ANY)
+    in_hbm = pl.BlockSpec(memory_space=pltpu.HBM)
     shape = (3, LAYERS, NODES)
     return pl.pallas_call(
         cell_kernel,
-        in_specs=[pl.BlockSpec(memory_space=pltpu.SMEM)] + [anywhere] * len(operands),
-        out_specs=[pl.BlockSpec(shape), pl.BlockSpec(shape), anywhere],
+        in_specs=[pl.BlockSpec(memory_space=pltpu.SMEM)] + [in_hbm] * len(operands),
+        out_specs=[pl.BlockSpec(shape), pl.BlockSpec(shape), in_hbm],
         out_shape=[
             jax.ShapeDtypeStruct(shape, f32),
             jax.ShapeDtypeStruct(shape, f32),
@@ -521,7 +521,7 @@
             pltpu.VMEM((6, 256, 256), bf16),
             pltpu.VMEM((6, 256, 256), f32),
         ],
-        compiler_params=pltpu.CompilerParams(vmem_limit_bytes=48 * 1024 * 1024),
+        compiler_params=pltpu.CompilerParams(vmem_limit_bytes=64 * 1024 * 1024),
         name="pier_step",
     )(count, *operands)
 

time: 44 us -> 36.8 us (0.84)
  local copies, waits for them, and re-layouts: 8.41 us -> 0 us
  other arithmetic: 0.61 us -> 1.33 us
  Pallas kernels: 18.6 us -> 19.1 us
    unnamed x20 -> x0, local copies, waits for them, and re-layouts: 8.41 us -> none
    add x1, other arithmetic: 0.61 us -> 1.33 us  [body(): return (own + shifted(low, -1), new_damage)]
    pallas_call x1, Pallas kernels: 18.6 us -> 19.1 us  [partition_step(): pl.pallas_call(cell_kernel, in_specs=[pl.BlockSpec(memory_space=pltpu.SME...]
where the time goes in v1:
time: 36.8 us; the launch traced here: 36.6 us
  Pallas kernels  19.1 us (52%)
  waiting for transfers between devices  9.5 us (26%)
  starting transfers between devices  5.32 us (14%)
  other arithmetic  1.33 us (4%)
  between operations  1.3 us (4%)
    pallas_call x1, Pallas kernels, partition_step(): pl.pallas_call(cell_kernel, in_specs=[pl.BlockSpec(memory_space=pltpu.SME...  19.1 us
    ppermute x2, waiting for transfers between devices, shifted(): return lax.ppermute(value, axes, pairs)  9.5 us
    ppermute x2, starting transfers between devices, shifted(): return lax.ppermute(value, axes, pairs)  5.32 us
    add x1, other arithmetic, body(): return (own + shifted(low, -1), new_damage)  1.33 us
  transfers between devices with their start and end apart: 2, of which 2 were waited for; matrix products, arithmetic and copies ran while one was open for 0% of the time, Pallas kernels for 0%

profile of v1, /device:TPU:32, one launch (start us, length us, event | category | flops | bytes accessed | tf_op | source)
XLA Modules:
  0.0 36.6 jit_solution(3741217748088166113)
XLA Ops:
  0.6 3.4 %collective-permute-start = (f32[3,4,289]{2,1,0:T(4,128)}, f32[3,4,289]{2,1,0:T(4,128)}, u32[]{:S(2)}, u32[]{:S(2)}) collective-permute-start(f32[3,4,289]{2,1,0:T(4,128)} %disp_hbm.1), channel_id=1, source_target_pairs={{0,1},{1,2},{2,3},{3,4},{4,5},{5,6},{6,7},{7,8},{8,9},{9,10},{10,1... | collective-permute-start | bytes 41624 | tf_op jit(solution)/shard_map/ppermute | solution.py:533
  4.7 5.6 %collective-permute-done.below_hbm = f32[3,4,289]{2,1,0:T(4,128)} collective-permute-done((f32[3,4,289]{2,1,0:T(4,128)}, f32[3,4,289]{2,1,0:T(4,128)}, u32[]{:S(2)}, u32[]{:S(2)}) %collective-permute-start) | collective-permute-done | bytes 13904 | tf_op jit(solution)/shard_map/ppermute | solution.py:533
  10.2 19.1 %pier_step.1 = (f32[3,4,289]{2,1,0:T(4,128)}, f32[3,4,289]{2,1,0:T(4,128)}, bf16[64,4096]{1,0:T(8,128)(2,1)}) custom-call(s32[1]{0:T(128)S(6)} %copy.13.count_ref, f32[3,4,289]{2,1,0:T(4,128)} %disp_hbm.1, f32[3,4,289]{2,1,0:T(4,128)} %collective-permute-done.below_hbm, f32[8,1024]{1,0:T(8,128)} %modulus_hbm.1, s32[1,64]{1,0:T(1,128)} %points_hbm.1, ...), custom_call_target="tpu_custom_call" | custom-call | tf_op jit(solution)/shard_map/pier_step/pallas_call | solution.py:497
  29.4 1.9 %collective-permute-start.1 = (f32[3,4,289]{2,1,0:T(4,128)}, f32[3,4,289]{2,1,0:T(4,128)S(1)}, u32[]{:S(2)}, u32[]{:S(2)}) collective-permute-start(f32[3,4,289]{2,1,0:T(4,128)} %get-tuple-element.6), channel_id=1, source_target_pairs={{1,0},{2,1},{3,2},{4,3},{5,4},{6,5},{7,6},{8,7},{9,8},{10,9},{11,1... | collective-permute-start | bytes 41624 | tf_op jit(solution)/shard_map/ppermute | solution.py:533
  31.3 3.9 %collective-permute-done.1 = f32[3,4,289]{2,1,0:T(4,128)S(1)} collective-permute-done((f32[3,4,289]{2,1,0:T(4,128)}, f32[3,4,289]{2,1,0:T(4,128)S(1)}, u32[]{:S(2)}, u32[]{:S(2)}) %collective-permute-start.1) | collective-permute-done | bytes 13904 | tf_op jit(solution)/shard_map/ppermute | solution.py:533
  35.2 1.3 %add.3 = f32[3,4,289]{2,1,0:T(4,128)} add(f32[3,4,289]{2,1,0:T(4,128)} %get-tuple-element.5, f32[3,4,289]{2,1,0:T(4,128)S(1)} %collective-permute-done.1) | non-fusion elementwise | flops 3468 | bytes 41616 | tf_op jit(solution)/shard_map/add | solution.py:541
Async XLA Ops:
  0.6 9.6 %collective-permute-start = (f32[3,4,289]{2,1,0:T(4,128)}, f32[3,4,289]{2,1,0:T(4,128)}, u32[]{:S(2)}, u32[]{:S(2)}) collective-permute-start(f32[3,4,289]{2,1,0:T(4,128)} %disp_hbm.1), channel_id=1, source_target_pairs={{0,1},{1,2},{2,3},{3,4},{4,5},{5,6},{6,7},{7,8},{8,9},{9,10},{10,1... | collective-permute-start | bytes 41624 | tf_op jit(solution)/shard_map/ppermute | solution.py:533
  29.4 5.9 %collective-permute-start.1 = (f32[3,4,289]{2,1,0:T(4,128)}, f32[3,4,289]{2,1,0:T(4,128)S(1)}, u32[]{:S(2)}, u32[]{:S(2)}) collective-permute-start(f32[3,4,289]{2,1,0:T(4,128)} %get-tuple-element.6), channel_id=1, source_target_pairs={{1,0},{2,1},{3,2},{4,3},{5,4},{6,5},{7,6},{8,7},{9,8},{10,9},{11,1... | collective-permute-start | bytes 41624 | tf_op jit(solution)/shard_map/ppermute | solution.py:533
